TPU v7x, 32 devices: a whole 2x2x4 slice. The times are simulated.
32 devices in a mesh: region: 16 (over z, y, x), blk: 2 (over core).
Axes of the slice: x: 2, y: 2, z: 4, core: 2. Of those that a mesh axis runs over, the one named last changes fastest.
Arguments:
- site_tensors: float32 [128, 2, 32, 1024], P('region', 'blk'), may hold values from -18 to 18
- projectors: bfloat16 [128, 2, 32, 1024], P('region'), may hold values from -0.1875 to 0.1875
- gate_matrix: float32 [2, 2, 2, 2], replicated, may hold values from -3 to 3
- recv_src: int32 [128, 3], P('region'), may hold values from 0 to 88, as said below
- cut_list: int32 [160], P('region'), may hold values from 0 to 23, as said below
- cut_dest: int32 [16, 10], replicated, may hold values from -1 to 63, as said below
- gate_src: int32 [128], P('region'), may hold values from 0 to 24, as said below
- gate_list: int32 [32], P('region'), may hold values from 0 to 7, as said below
- gate_dest: int32 [16, 2], replicated, may hold values from -1 to 15, as said below
Outputs:
- new_sites: float32 [128, 2, 32, 1024], P('region', 'blk')
- messages: float32 [128, 3, 1024], P('region')
Inputs may be any that keep to these rules, and one draw needn't show every extreme that they name: `recv_src`: messages between one ordered pair of regions use distinct slots below 4; some pair uses all 4. `cut_list`: entries whose cut_dest is -1 are padding. `cut_dest`: some region fills all 10 entries of its row. `gate_src`: gate partners form pairs along vertical links. `gate_list`: entries whose gate_dest is -1 are padding. `gate_dest`: some region fills all 2 entries of its row.
All inputs are finite; a program needn't handle non-finite values.
Results may differ from a plain program's by a relative error of at most 0.0039.
Values may be sent and summed in bfloat16 or wider, within the bound.
A program may use at most 128 MiB of HBM per device.

v0:
```python
import jax
import jax.numpy as jnp
from jax import lax
from jax.sharding import PartitionSpec as P

SWEEPS = 2
CAP = 4
GCAP = 1


HIGHEST = lax.Precision.HIGHEST
EPSILON = 1e-06


def weighted(tensors, incoming):
    partial_a = jnp.einsum("isabc,iag->isgbc", tensors, incoming[:, 0], precision=HIGHEST)
    return jnp.einsum("isgbc,ibe->isgec", partial_a, incoming[:, 1], precision=HIGHEST)


def outgoing(tensors, incoming):
    partial_c = jnp.einsum("isabc,icd->isabd", tensors, incoming[:, 2], precision=HIGHEST)
    both_bc = jnp.einsum("isabd,ibe->isaed", partial_c, incoming[:, 1], precision=HIGHEST)
    leg_zero = jnp.einsum("isaed,isfed->iaf", both_bc, tensors, precision=HIGHEST)
    both_ac = jnp.einsum("isabd,iag->isgbd", partial_c, incoming[:, 0], precision=HIGHEST)
    leg_one = jnp.einsum("isgbd,isghd->ibh", both_ac, tensors, precision=HIGHEST)
    both_ab = weighted(tensors, incoming)
    leg_two = jnp.einsum("isgec,isgek->ick", both_ab, tensors, precision=HIGHEST)
    return jnp.stack([leg_zero, leg_one, leg_two], axis=1)


def normalized(leg_terms):
    trace_sum = jnp.trace(leg_terms, axis1=2, axis2=3)
    return leg_terms.shape[-1] * leg_terms / trace_sum[:, :, None, None]


def select_rows(dest_table, my_region, capacity):
    region_count, columns = dest_table.shape
    wanted = my_region * capacity + jnp.arange(capacity, dtype=jnp.int32)
    matched = dest_table[:, :, None] == wanted[None, None, :]
    position = jnp.sum(
        jnp.where(matched, jnp.arange(columns, dtype=jnp.int32)[None, :, None], 0), axis=1
    )
    return (jnp.arange(region_count, dtype=jnp.int32)[:, None] * columns + position).reshape(-1)


def shards(
    site_tensors,
    projectors,
    gate_matrix,
    recv_src,
    cut_list,
    cut_dest,
    gate_src,
    gate_list,
    gate_dest,
):
    site_count = site_tensors.shape[0]
    bond_dim = site_tensors.shape[2]
    regions = lax.axis_size("region")
    my_region = lax.axis_index("region")
    my_spin = lax.axis_index("blk")
    tensors = site_tensors.reshape(site_count, 1, bond_dim, bond_dim, bond_dim)
    boundary = jnp.zeros((bond_dim, bond_dim), jnp.float32).at[0, 0].set(bond_dim)
    identity = jnp.eye(bond_dim, dtype=jnp.float32)
    msg_none = 3 * site_count + regions * CAP
    incoming = jnp.where((recv_src == msg_none)[:, :, None, None], boundary, identity)
    edge_row = boundary.reshape(1, bond_dim * bond_dim)
    for sweep_index in range(SWEEPS):
        totals = lax.psum(outgoing(tensors, incoming), "blk")
        fresh_msgs = normalized(totals).reshape(3 * site_count, bond_dim * bond_dim)
        leaving = fresh_msgs[cut_list]
        everyone = lax.all_gather(leaving, "region", axis=0, tiled=True)
        arrived = everyone[select_rows(cut_dest, my_region, CAP)]
        lookup = jnp.concatenate([fresh_msgs, arrived, edge_row], axis=0)
        incoming = lookup[recv_src].reshape(site_count, 3, bond_dim, bond_dim)
    messages = incoming.reshape(site_count, 3, bond_dim * bond_dim)
    weights = (
        weighted(tensors, incoming)
        .astype(jnp.bfloat16)
        .reshape(site_count, bond_dim * bond_dim, bond_dim)
    )
    factor = jnp.einsum(
        "ikc,isnk->icsn", weights, projectors, preferred_element_type=jnp.float32
    ).astype(jnp.bfloat16)
    factor = factor.reshape(site_count, 1, bond_dim, 2 * bond_dim)
    halves = lax.all_gather(factor, "blk", axis=1, tiled=True)
    flat_factor = halves.reshape(site_count, 4 * bond_dim * bond_dim)
    leaving_factor = flat_factor[gate_list]
    everyone_factor = lax.all_gather(leaving_factor, "region", axis=0, tiled=True)
    arrived_factor = everyone_factor[select_rows(gate_dest, my_region, GCAP)]
    empty_row = jnp.zeros((1, 4 * bond_dim * bond_dim), jnp.bfloat16)
    factor_lookup = jnp.concatenate([flat_factor, arrived_factor, empty_row], axis=0)
    partners = factor_lookup[gate_src].reshape(site_count, 2, bond_dim, 2, bond_dim)
    mixing = jnp.einsum(
        "ajby,iycjn->iabcn", gate_matrix, partners.astype(jnp.float32), precision=HIGHEST
    )
    own_old = lax.dynamic_index_in_dim(mixing, my_spin, 2, keepdims=False)
    spin_piece = jnp.einsum("iuvc,iacn->iauvn", tensors[:, 0], own_old, precision=HIGHEST)
    spin_piece = spin_piece.reshape(site_count, 2, bond_dim, bond_dim * bond_dim)
    summed = lax.psum_scatter(spin_piece, "blk", scatter_dimension=1, tiled=True)
    squares = jnp.sum(summed * summed, axis=(1, 2, 3))
    total_sq = lax.psum(squares, "blk")
    mean_sq = total_sq / (2 * bond_dim**3)
    updated = summed / jnp.sqrt(mean_sq + EPSILON)[:, None, None, None]
    unchanged = gate_src == site_count + regions * GCAP
    new_sites = jnp.where(unchanged[:, None, None, None], site_tensors, updated)
    return (new_sites, messages)


def solution(mesh):
    return jax.shard_map(
        shards,
        mesh=mesh,
        in_specs=(
            P("region", "blk", None, None),
            P("region", None, None, None),
            P(),
            P("region", None),
            P("region"),
            P(),
            P("region"),
            P("region"),
            P(),
        ),
        out_specs=(P("region", "blk", None, None), P("region", None, None)),
        check_vma=False,
    )
```

profile of v0, /device:TPU:0, one launch (start us, length us, event | category | flops | bytes accessed | tf_op | source)
XLA Modules:
  0.0 483.5 jit_solution(1316465474755128273)
XLA Ops:
  8.0 3.9 reshape.220
  11.9 6.4 %copy.94 = f32[8,32,32,32]{2,1,3,0:T(8,128)} copy(f32[8,32,32,32]{3,2,1,0:T(8,128)} %reshape.220) | data formatting | bytes 2097152 | tf_op jit(solution)/shard_map/reshape.47
  18.4 20.8 %convolution_bitcast_fusion.3 = f32[8,32,32,32]{2,3,1,0:T(8,128)S(1)} fusion(f32[8,32,32,32]{3,2,1,0:T(8,128)} %reshape.220, f32[8,3,32,32]{2,3,0,1:T(8,128)S(1)} %broadcast_select_fusion), kind=kOutput, calls=%fused_computation.35 | convolution fusion | flops 100663296 | bytes 2228224 | tf_op jit(solution)/shard_map/isabc,icd->isabd/dot_general | solution.py:21
  39.2 9.3 %fusion.14 = f32[8,32,32,32]{1,2,3,0:T(8,128)} fusion(f32[8,32,32,32]{2,3,1,0:T(8,128)S(1)} %convolution_bitcast_fusion.3, f32[8,3,32,32]{2,3,0,1:T(8,128)S(1)} %broadcast_select_fusion), kind=kOutput, calls=%fused_computation.23 | convolution fusion | flops 100663296 | bytes 5373952 | tf_op jit(solution)/shard_map/isabd,iag->isgbd/dot_general | solution.py:24
  48.5 20.7 %convolution_bitcast_fusion.2 = f32[8,32,32,32]{3,2,1,0:T(8,128)} fusion(f32[8,32,32,32]{2,3,1,0:T(8,128)S(1)} %convolution_bitcast_fusion.3, f32[8,3,32,32]{2,3,0,1:T(8,128)S(1)} %broadcast_select_fusion), kind=kOutput, calls=%fused_computation.34 | convolution fusion | flops 100663296 | bytes 5373952 | tf_op jit(solution)/shard_map/isabd,ibe->isaed/dot_general | solution.py:22
  69.2 6.8 %fusion.20 = f32[8,32,32,32]{3,1,2,0:T(8,128)} fusion(f32[8,32,32,32]{3,2,1,0:T(8,128)S(1)} %copy-done.1, f32[8,3,32,32]{2,3,0,1:T(8,128)S(1)} %broadcast_select_fusion), kind=kOutput, calls=%fused_computation.29 | convolution fusion | flops 100663296 | bytes 5373952 | tf_op jit(solution)/shard_map/isabc,iag->isgbc/dot_general | solution.py:16
  76.0 6.8 %copy.93 = f32[8,32,32,32]{2,1,3,0:T(8,128)} copy(f32[8,32,32,32]{3,2,1,0:T(8,128)} %convolution_bitcast_fusion.2) | data formatting | bytes 2097152 | tf_op jit(solution)/shard_map/reshape.51
  82.8 9.8 %convolution_bitcast_fusion.7 = f32[8,1,32,32]{3,2,0,1:T(8,128)S(1)} fusion(f32[8,32,32,32]{1,2,3,0:T(8,128)} %fusion.14, f32[8,32,32,32]{2,1,3,0:T(8,128)} %copy.94), kind=kOutput, calls=%fused_computation.43 | convolution fusion | flops 100663296 | bytes 2129920 | tf_op jit(solution)/shard_map/isgbd,isghd->ibh/dot_general | solution.py:25
  92.6 4.1 convolution_bitcast_fusion.8
  96.7 6.3 %fusion.12 = f32[8,32,32,32]{3,1,2,0:T(8,128)S(1)} fusion(f32[8,32,32,32]{3,1,2,0:T(8,128)S(1)} %copy-done.8, f32[8,3,32,32]{2,3,0,1:T(8,128)S(1)} %broadcast_select_fusion), kind=kOutput, calls=%fused_computation.21 | convolution fusion | flops 100663296 | bytes 5373952 | tf_op jit(solution)/shard_map/isgbc,ibe->isgec/dot_general | solution.py:17
  103.1 7.0 %fusion.28 = f32[8,1,32,32]{3,2,0,1:T(8,128)S(1)} fusion(f32[8,32,32,32]{3,2,1,0:T(8,128)S(1)} %copy-done.2, f32[8,32,32,32]{3,1,2,0:T(8,128)S(1)} %fusion.12), kind=kOutput, calls=%fused_computation.39 | convolution fusion | flops 100663296 | bytes 2129920 | tf_op jit(solution)/shard_map/isgec,isgek->ick/dot_general | solution.py:27
  114.8 17.5 %all-reduce.5.cloned.1.call-done = f32[8,3,32,32]{3,2,0,1:T(8,128)} async-done(((f32[8,3,32,32]{3,2,0,1:T(8,128)}), f32[8,3,32,32]{3,2,0,1:T(8,128)}) %all-reduce.5.cloned.1.call-update) | async-done | bytes 98320 | tf_op jit(solution)/shard_map/psum | solution.py:69
  135.3 49.6 %all-gather.3 = f32[16,10,1024]{2,1,0:T(8,128)} all-gather(f32[1,10,1024]{2,1,0:T(8,128)S(1)} %bitcast.197), channel_id=2, replica_groups=mesh['region'=16,'blk'=2] {'region'}, dimensions={0}, use_global_device_ids=true | all-gather | bytes 696320 | tf_op jit(solution)/shard_map/all_gather | solution.py:72
  187.7 21.5 %convolution_bitcast_fusion.1 = f32[8,32,32,32]{2,3,1,0:T(8,128)S(1)} fusion(f32[8,32,32,32]{3,2,1,0:T(8,128)} %reshape.220, f32[8,3,32,32]{3,2,1,0:T(8,128)S(1)} %reshape.224), kind=kOutput, calls=%fused_computation.33 | convolution fusion | flops 100663296 | bytes 2228224 | tf_op jit(solution)/shard_map/isabc,icd->isabd/dot_general | solution.py:21
  209.2 8.4 %fusion.10 = f32[8,32,32,32]{1,2,3,0:T(8,128)S(1)} fusion(f32[8,32,32,32]{2,3,1,0:T(8,128)S(1)} %convolution_bitcast_fusion.1, f32[8,3,32,32]{3,2,1,0:T(8,128)S(1)} %reshape.224), kind=kOutput, calls=%fused_computation.19 | convolution fusion | flops 100663296 | bytes 5373952 | tf_op jit(solution)/shard_map/isabd,iag->isgbd/dot_general | solution.py:24
  217.6 20.9 %convolution_bitcast_fusion = f32[8,32,32,32]{3,2,1,0:T(8,128)} fusion(f32[8,32,32,32]{2,3,1,0:T(8,128)S(1)} %convolution_bitcast_fusion.1, f32[8,3,32,32]{3,2,1,0:T(8,128)S(1)} %reshape.224), kind=kOutput, calls=%fused_computation.32 | convolution fusion | flops 100663296 | bytes 5373952 | tf_op jit(solution)/shard_map/isabd,ibe->isaed/dot_general | solution.py:22
  238.5 6.9 %fusion.18 = f32[8,32,32,32]{3,1,2,0:T(8,128)} fusion(f32[8,32,32,32]{3,2,1,0:T(8,128)S(1)} %copy-done.3, f32[8,3,32,32]{3,2,1,0:T(8,128)S(1)} %reshape.224), kind=kOutput, calls=%fused_computation.27 | convolution fusion | flops 100663296 | bytes 5373952 | tf_op jit(solution)/shard_map/isabc,iag->isgbc/dot_general | solution.py:16
  245.4 6.3 %convolution_bitcast_fusion.5 = f32[8,1,32,32]{3,2,0,1:T(8,128)S(1)} fusion(f32[8,32,32,32]{1,2,3,0:T(8,128)S(1)} %fusion.10, f32[8,32,32,32]{2,1,3,0:T(8,128)S(1)} %copy-done.6), kind=kOutput, calls=%fused_computation.41 | convolution fusion | flops 100663296 | bytes 2129920 | tf_op jit(solution)/shard_map/isgbd,isghd->ibh/dot_general | solution.py:25
  251.7 6.8 %copy.109 = f32[8,32,32,32]{2,1,3,0:T(8,128)} copy(f32[8,32,32,32]{3,2,1,0:T(8,128)} %convolution_bitcast_fusion) | data formatting | bytes 2097152 | tf_op jit(solution)/shard_map/reshape.70
  258.5 7.7 %convolution_bitcast_fusion.6 = f32[8,1,32,32]{3,2,0,1:T(8,128)S(1)} fusion(f32[8,32,32,32]{2,1,3,0:T(8,128)} %copy.109, f32[8,32,32,32]{2,1,3,0:T(8,128)} %copy.94), kind=kOutput, calls=%fused_computation.42 | convolution fusion | flops 100663296 | bytes 2129920 | tf_op jit(solution)/shard_map/isaed,isfed->iaf/dot_general | solution.py:23
  266.2 6.2 %fusion.8 = f32[8,32,32,32]{3,1,2,0:T(8,128)S(1)} fusion(f32[8,32,32,32]{3,1,2,0:T(8,128)S(1)} %copy-done.7, f32[8,3,32,32]{3,2,1,0:T(8,128)S(1)} %reshape.224), kind=kOutput, calls=%fused_computation.17 | convolution fusion | flops 100663296 | bytes 5373952 | tf_op jit(solution)/shard_map/isgbc,ibe->isgec/dot_general | solution.py:17
  272.4 7.1 %fusion.31 = f32[8,1,32,32]{3,2,0,1:T(8,128)S(1)} fusion(f32[8,32,32,32]{3,2,1,0:T(8,128)S(1)} %copy-done.4, f32[8,32,32,32]{3,1,2,0:T(8,128)S(1)} %fusion.8), kind=kOutput, calls=%fused_computation.40 | convolution fusion | flops 100663296 | bytes 2129920 | tf_op jit(solution)/shard_map/isgec,isgek->ick/dot_general | solution.py:27
  280.4 14.5 %all-reduce.7.cloned.1.call-done = f32[8,3,32,32]{3,2,0,1:T(8,128)} async-done(((f32[8,3,32,32]{3,2,0,1:T(8,128)}), f32[8,3,32,32]{3,2,0,1:T(8,128)}) %all-reduce.7.cloned.1.call-update) | async-done | bytes 98320 | tf_op jit(solution)/shard_map/psum | solution.py:69
  297.9 49.6 %all-gather.4 = f32[16,10,1024]{2,1,0:T(8,128)} all-gather(f32[1,10,1024]{2,1,0:T(8,128)S(1)} %bitcast.196), channel_id=3, replica_groups=mesh['region'=16,'blk'=2] {'region'}, dimensions={0}, use_global_device_ids=true | all-gather | bytes 696320 | tf_op jit(solution)/shard_map/all_gather | solution.py:72
  350.3 8.3 %fusion.16 = f32[8,32,32,32]{3,1,2,0:T(8,128)S(1)} fusion(f32[8,32,32,32]{3,2,1,0:T(8,128)} %reshape.220, f32[8,3,32,32]{3,2,1,0:T(8,128)S(1)} %reshape.228), kind=kOutput, calls=%fused_computation.25 | convolution fusion | flops 100663296 | bytes 2228224 | tf_op jit(solution)/shard_map/isabc,iag->isgbc/dot_general | solution.py:16
  358.6 5.6 %fusion.25 = bf16[8,32,32,32]{3,1,2,0:T(8,128)(2,1)S(1)} fusion(f32[8,32,32,32]{3,1,2,0:T(8,128)S(1)} %fusion.16, f32[8,3,32,32]{3,2,1,0:T(8,128)S(1)} %reshape.228), kind=kOutput, calls=%fused_computation.36 | convolution fusion | flops 100925440 | bytes 4849664 | tf_op jit(solution)/shard_map/isgbc,ibe->isgec/dot_general | solution.py:17
  368.3 37.0 %all-gather.5 = bf16[16,2,4096]{2,1,0:T(2,128)(2,1)S(1)} all-gather(bf16[1,2,4096]{2,1,0:T(2,128)(2,1)S(1)} %bitcast.198), channel_id=4, replica_groups=mesh['region'=16,'blk'=2] {'region'}, dimensions={0}, use_global_device_ids=true | all-gather | bytes 278528 | tf_op jit(solution)/shard_map/all_gather | solution.py:89
  408.3 24.5 %fusion.22 = f32[8,2,32,32,32]{3,4,2,1,0:T(8,128)} fusion(f32[8,32,32,32,1]{3,2,1,0,4:T(8,128)} %reshape.344, f32[8,2,32,32,1]{3,1,2,0,4:T(2,128)S(1)} %bitcast.195), kind=kOutput, calls=%fused_computation.31 | convolution fusion | flops 201326592 | bytes 3211264 | tf_op jit(solution)/shard_map/iuvc,iacn->iauvn/dot_general | solution.py:98
  432.8 9.0 %copy.129 = f32[8,2,32,32,32]{4,3,2,1,0:T(8,128)} copy(f32[8,2,32,32,32]{3,4,2,1,0:T(8,128)} %fusion.22) | data formatting | bytes 4194304 | tf_op jit(solution)/shard_map/iuvc,iacn->iauvn/transpose | solution.py:98
  441.8 7.7 %reshape.233 = f32[8,2,32,1024]{3,2,1,0:T(8,128)} reshape(f32[8,2,32,32,32]{4,3,2,1,0:T(8,128)} %copy.129) | data formatting | bytes 4194304 | tf_op jit(solution)/shard_map/reshape | solution.py:99
  450.1 18.5 %all-reduce.9.cloned.1.call-done = f32[8,2,32,1024]{3,2,1,0:T(8,128)} async-done(((f32[8,2,32,1024]{3,2,1,0:T(8,128)}), f32[8,2,32,1024]{3,2,1,0:T(8,128)}) %all-reduce.9.cloned.1.call-update) | async-done | bytes 2097168
  473.8 3.0 divide_select_fusion
  (121 shorter events, 30.6 us)
Async XLA Ops:
  7.2 357.1 %copy-start = (bf16[8,2,32,1024]{3,2,1,0:T(8,128)(2,1)S(1)}, bf16[8,2,32,1024]{3,2,1,0:T(8,128)(2,1)}, u32[]{:S(2)}) copy-start(bf16[8,2,32,1024]{3,2,1,0:T(8,128)(2,1)} %param.12) | copy-start | bytes 3145732
  7.2 125.1 %all-reduce.5.cloned.1.call-start = ((), (), s32[]{:S(2)}) async-start(), calls=%async_computation | async-start | bytes 786432 | tf_op jit(solution)/shard_map/psum | solution.py:69
  11.9 6.4 %copy-start.12 = (f32[32,32]{0,1:T(8,128)S(1)}, f32[32,32]{0,1:T(8,128)}, u32[]{:S(2)}) copy-start(f32[32,32]{0,1:T(8,128)} %constant.75.clone.1) | copy-start | bytes 12292
  48.5 20.7 %copy-start.1 = (f32[8,32,32,32]{3,2,1,0:T(8,128)S(1)}, f32[8,32,32,32]{3,2,1,0:T(8,128)}, u32[]{:S(2)}) copy-start(f32[8,32,32,32]{3,2,1,0:T(8,128)} %reshape.220) | copy-start | bytes 3145732
  82.8 9.8 %copy-start.5 = (f32[8,32,32,32]{2,1,3,0:T(8,128)S(1)}, f32[8,32,32,32]{2,1,3,0:T(8,128)}, u32[]{:S(2)}) copy-start(f32[8,32,32,32]{2,1,3,0:T(8,128)} %copy.94) | copy-start | bytes 3145732
  82.8 9.8 %copy-start.9 = (f32[8,32,32,32]{2,1,3,0:T(8,128)S(1)}, f32[8,32,32,32]{2,1,3,0:T(8,128)}, u32[]{:S(2)}) copy-start(f32[8,32,32,32]{2,1,3,0:T(8,128)} %copy.93) | copy-start | bytes 3145732
  92.6 4.1 copy-start.8
  96.7 6.4 %copy-start.2 = (f32[8,32,32,32]{3,2,1,0:T(8,128)S(1)}, f32[8,32,32,32]{3,2,1,0:T(8,128)}, u32[]{:S(2)}) copy-start(f32[8,32,32,32]{3,2,1,0:T(8,128)} %reshape.220) | copy-start | bytes 3145732
  103.1 7.9 %copy-start.13 = (s32[8,3]{0,1:T(4,128)S(1)}, s32[8,3]{0,1:T(4,128)}, u32[]{:S(2)}) copy-start(s32[8,3]{0,1:T(4,128)} %param.14) | copy-start | bytes 292
  103.1 8.0 %copy-start.10 = (f32[8,1,32,1024]{3,2,1,0:T(8,128)S(1)}, f32[8,1,32,1024]{3,2,1,0:T(8,128)}, u32[]{:S(2)}) copy-start(f32[8,1,32,1024]{3,2,1,0:T(8,128)} %param.11) | copy-start | bytes 3145732
  110.1 3.7 copy-start.16
  110.1 3.7 copy-start.17
  110.1 3.8 copy-start.18
  110.1 3.8 copy-start.19
  110.1 4.0 copy-start.15
  110.1 4.2 copy-start.14
  110.9 183.9 %all-reduce.7.cloned.1.call-start = ((), (), s32[]{:S(2)}) async-start(), calls=%async_computation.1 | async-start | bytes 786432 | tf_op jit(solution)/shard_map/psum | solution.py:69
  113.8 73.2 %copy-start.11 = (f32[1,1024]{1,0:T(1,128)S(1)}, f32[1,1024]{1,0:T(1,128)}, u32[]{:S(2)}) copy-start(f32[1,1024]{1,0:T(1,128)} %constant.84.clone.1) | copy-start | bytes 12292
  217.6 20.9 %copy-start.3 = (f32[8,32,32,32]{3,2,1,0:T(8,128)S(1)}, f32[8,32,32,32]{3,2,1,0:T(8,128)}, u32[]{:S(2)}) copy-start(f32[8,32,32,32]{3,2,1,0:T(8,128)} %reshape.220) | copy-start | bytes 3145732
  238.5 6.9 %copy-start.6 = (f32[8,32,32,32]{2,1,3,0:T(8,128)S(1)}, f32[8,32,32,32]{2,1,3,0:T(8,128)}, u32[]{:S(2)}) copy-start(f32[8,32,32,32]{2,1,3,0:T(8,128)} %copy.94) | copy-start | bytes 3145732
  258.4 7.7 %copy-start.7 = (f32[8,32,32,32]{3,1,2,0:T(8,128)S(1)}, f32[8,32,32,32]{3,1,2,0:T(8,128)}, u32[]{:S(2)}) copy-start(f32[8,32,32,32]{3,1,2,0:T(8,128)} %fusion.18) | copy-start | bytes 3145732
  266.2 6.2 %copy-start.4 = (f32[8,32,32,32]{3,2,1,0:T(8,128)S(1)}, f32[8,32,32,32]{3,2,1,0:T(8,128)}, u32[]{:S(2)}) copy-start(f32[8,32,32,32]{3,2,1,0:T(8,128)} %reshape.220) | copy-start | bytes 3145732
  280.4 188.3 %all-reduce.9.cloned.1.call-start = ((), (), s32[]{:S(2)}) async-start(), calls=%async_computation.2 | async-start | bytes 4194304
  441.8 7.7 %copy-start.20 = (u32[32]{0:T(128)S(1)}, u32[32]{0:T(128)}, u32[]{:S(2)}) copy-start(u32[32]{0:T(128)} %constant.101) | copy-start | bytes 388
Sparse Core Ops, SparseCore 0:
  111.1 21.1 all-reduce.4
  280.5 14.3 all-reduce.6
  449.6 18.9 all-reduce.8
where the time goes:
time: 492 us; the launch traced here: 484 us
  matrix products  210 us (43%)
  blocking collectives  141 us (29%)
  local copies, waits for them, and re-layouts  55.2 us (11%)
  waiting for transfers between devices  50.5 us (10%)
  between operations  14.6 us (3%)
  other arithmetic  12.3 us (2%)
    all_gather x2, blocking collectives, shards(): everyone = lax.all_gather(leaving, 'region', axis=0, tiled=True)  99.2 us
    dot_general x2, matrix products, outgoing(): jnp.einsum('isabc,icd->isabd', tensors, incoming[:, 2], precision=HIGHEST)  42.2 us
    dot_general x2, matrix products, outgoing(): jnp.einsum('isabd,ibe->isaed', partial_c, incoming[:, 1], precision=HIGHEST)  41.6 us
    all_gather x1, blocking collectives, shards(): lax.all_gather(leaving_factor, 'region', axis=0, tiled=True)  37 us
    psum x2, waiting for transfers between devices, shards(): totals = lax.psum(outgoing(tensors, incoming), 'blk')  32 us
    another operation x6, local copies, waits for them, and re-layouts  26.8 us
    dot_general x1, matrix products, shards(): jnp.einsum('iuvc,iacn->iauvn', tensors[:, 0], own_old, precision=HIGHEST)  24.5 us
    dot_general x3, matrix products, weighted(): jnp.einsum('isabc,iag->isgbc', tensors, incoming[:, 0], precision=HIGHEST)  22.1 us
  transfers between devices with their start and end apart: 3, of which 3 were waited for; matrix products, arithmetic and copies ran while one was open for 1% of the time, Pallas kernels for 0%

commit v1 on v0

v1 whole, which is shorter than its diff:
```python
import functools

import jax
import jax.numpy as jnp
from jax import lax
from jax.experimental import pallas as pl
from jax.experimental.pallas import tpu as pltpu
from jax.sharding import PartitionSpec as P

SWEEPS = 2
CAP = 4
GCAP = 1
EPSILON = 1e-06
VMEM = pl.BlockSpec(memory_space=pltpu.VMEM)
SMEM = pl.BlockSpec(memory_space=pltpu.SMEM)
MESH = pl.DeviceIdType.MESH


def split(value):
    high = value.astype(jnp.bfloat16)
    low = (value - high.astype(jnp.float32)).astype(jnp.bfloat16)
    return high, low


def contract(left, right, dims):
    dot = functools.partial(
        lax.dot_general,
        dimension_numbers=(dims, ((), ())),
        preferred_element_type=jnp.float32,
    )
    return dot(left[0], right[0]) + (dot(left[1], right[0]) + dot(left[0], right[1]))


def chunks(rows):
    return jnp.concatenate(
        [rows[:, 128 * j : 128 * (j + 1)] for j in range(rows.shape[1] // 128)], axis=0
    )


def unchunk(stacked, bond):
    return jnp.concatenate(
        [stacked[bond * j : bond * (j + 1)] for j in range(stacked.shape[0] // bond)], axis=1
    )


def swap_axes(stacked, source, target, bond):
    per = 128 // bond
    groups = bond // per
    source[...] = stacked
    lane = lax.broadcasted_iota(jnp.int32, (groups * groups, 128), 1) // bond
    taken = [
        jnp.concatenate(
            [source[pl.ds(per * k + q, groups, stride=bond), :] for k in range(groups)], axis=0
        )
        for q in range(per)
    ]
    for p in range(per):
        merged = taken[p]
        for q in range(per):
            if q != p:
                moved = pltpu.roll(taken[q], (bond * (q - p)) % 128, 1)
                merged = jnp.where(lane == q, moved, merged)
        for k in range(groups):
            target[pl.ds(bond * k + p, groups, stride=per), :] = merged[
                groups * k : groups * (k + 1)
            ]
    return target[...]


def diagonal(matrix):
    bond = matrix.shape[0]
    per = 128 // bond
    wide = jnp.concatenate([matrix] * per, axis=1)
    tall = jnp.concatenate([wide] * per, axis=0)
    row = lax.broadcasted_iota(jnp.int32, (128, 128), 0) // bond
    column = lax.broadcasted_iota(jnp.int32, (128, 128), 1) // bond
    return jnp.where(row == column, tall, 0.0)


def slots(entries, dest_row, count):
    matched = dest_row[None, :] == jnp.arange(count, dtype=jnp.int32)[:, None]
    return jnp.sum(jnp.where(matched, entries[None, :], 0), axis=1).astype(jnp.int32)


def site_terms(tensors, current, site, swaps):
    bond = tensors.shape[1]
    rows, inner, outer = ((1,), (0,)), ((1,), (1,)), ((0,), (0,))
    wide = tensors[site]
    plain = chunks(wide)
    swapped = swap_axes(plain, swaps.at[0], swaps.at[1], bond)
    left = split(current[3 * site][:, :bond])
    right = split(current[3 * site + 1][:, :bond])
    vertical = split(diagonal(current[3 * site + 2][:, :bond]))
    on_a = contract(left, split(wide), outer)
    on_b = contract(right, split(unchunk(swapped, bond)), outer)
    on_a_stacked = chunks(on_a)
    on_a_swapped = unchunk(swap_axes(on_a_stacked, swaps.at[2], swaps.at[3], bond), bond)
    on_b_stacked = swap_axes(chunks(on_b), swaps.at[4], swaps.at[5], bond)
    on_b_swapped = unchunk(on_b_stacked, bond)
    on_c = unchunk(contract(split(plain), vertical, rows), bond)
    on_c_swapped = unchunk(contract(split(swapped), vertical, rows), bond)
    leg_zero = contract(split(on_b_swapped), split(on_c), inner)
    leg_one = contract(split(on_a_swapped), split(on_c_swapped), inner)
    crossed = contract(split(on_a_stacked), split(on_b_stacked), outer)
    crossed = jnp.where(same_block(bond), crossed, 0.0)
    folded = sum(crossed[bond * p : bond * (p + 1)] for p in range(128 // bond))
    return leg_zero, leg_one, fold_lanes(folded)[:, :bond]


def same_block(bond):
    row = lax.broadcasted_iota(jnp.int32, (128, 128), 0) // bond
    column = lax.broadcasted_iota(jnp.int32, (128, 128), 1) // bond
    return row == column


def fold_lanes(value):
    value = value + pltpu.roll(value, 64, 1)
    return value + pltpu.roll(value, 32, 1)


def flatten(matrix, scratch):
    bond = matrix.shape[0]
    per = 128 // bond
    scratch[...] = jnp.concatenate([matrix] * per, axis=1)
    lane = lax.broadcasted_iota(jnp.int32, (bond // per, 128), 1) // bond
    flat = scratch[pl.ds(0, bond // per, stride=per), :]
    for p in range(1, per):
        flat = jnp.where(lane == p, scratch[pl.ds(p, bond // per, stride=per), :], flat)
    return flat


def whole_kernel(
    regions,
    send_index,
    recv_src,
    gate_index,
    gate_src,
    gate,
    tensors,
    projectors,
    edge,
    new_out,
    msg_out,
    current,
    swaps,
    flats,
    partial,
    mate,
    lookup,
    outbox,
    arrived,
    factors,
    gate_outbox,
    gate_arrived,
    both,
    half,
    own,
    update_outbox,
    update_inbox,
    squares,
    norms,
    mate_sem,
    send_sem,
    recv_sem,
    gate_send_sem,
    gate_recv_sem,
    update_send_sem,
    update_recv_sem,
):
    me = lax.axis_index("region")
    core = lax.axis_index("blk")
    sites, bond, width = tensors.shape
    per = 128 // bond
    pieces = width // 128
    messages = 3 * sites
    none = messages + regions * CAP
    barrier = pltpu.get_barrier_semaphore()
    pl.semaphore_signal(barrier, inc=1, device_id=(me, 1 - core), device_id_type=MESH)

    def hello(step, carry):
        other = lax.rem(me + step, regions)
        pl.semaphore_signal(barrier, inc=1, device_id=(other, core), device_id_type=MESH)
        return carry

    lax.fori_loop(1, regions, hello, 0)

    def to_mate(source, target, index):
        return pltpu.make_async_remote_copy(
            src_ref=source,
            dst_ref=target,
            send_sem=mate_sem.at[2 * index],
            recv_sem=mate_sem.at[2 * index + 1],
            device_id=(me, 1 - core),
            device_id_type=MESH,
        )

    def unflatten(flat, entry):
        for p in range(per):
            moved = flat if p == 0 else pltpu.roll(flat, 128 - bond * p, 1)
            current[entry, pl.ds(p, bond // per, stride=per), :] = moved

    row = lax.broadcasted_iota(jnp.int32, (8, 128), 0)
    column = lax.broadcasted_iota(jnp.int32, (8, 128), 1)
    place = 128 * row + column
    diagonal_flat = (place // bond) == (place % bond)
    identity = jnp.where(diagonal_flat, 1.0, 0.0).astype(jnp.float32)

    def begin(entry, carry):
        unflatten(jnp.where(recv_src[entry] == none, edge[...], identity), entry)
        return carry

    lax.fori_loop(0, messages, begin, 0)

    for sweep in range(SWEEPS):

        def terms(site, carry, sweep=sweep):
            legs = site_terms(tensors, current, site, swaps)
            for leg in range(3):
                partial[sweep, 3 * site + leg] = flatten(legs[leg], flats.at[leg])
            return carry

        lax.fori_loop(0, sites, terms, 0)
        if sweep == 0:
            pl.semaphore_wait(barrier, regions)
        swap = to_mate(partial.at[sweep], mate.at[sweep], sweep)
        swap.start()
        swap.wait()
        total = partial[sweep] + mate[sweep]
        trace = jnp.sum(jnp.where(diagonal_flat[None], total, 0.0), axis=(1, 2), keepdims=True)
        lookup[pl.ds(0, messages)] = bond * total / trace

        def remote(other, slot, sweep=sweep):
            return pltpu.make_async_remote_copy(
                src_ref=outbox.at[sweep, other],
                dst_ref=arrived.at[sweep, slot],
                send_sem=send_sem.at[sweep, other],
                recv_sem=recv_sem.at[sweep, slot],
                device_id=(other, core),
                device_id_type=MESH,
            )

        def send(step, carry, sweep=sweep, remote=remote):
            other = lax.rem(me + step, regions)
            for slot in range(CAP):
                outbox[sweep, other, slot] = lookup[send_index[CAP * other + slot]]
            remote(other, me).start()
            return carry

        lax.fori_loop(1, regions, send, 0)
        arrived[sweep, me] = jnp.zeros_like(arrived[sweep, me])

        def collect(step, carry, remote=remote):
            other = lax.rem(me + step, regions)
            remote(other, me).wait_send()
            remote(other, other).wait_recv()
            return carry

        lax.fori_loop(1, regions, collect, 0)
        lookup[pl.ds(messages, regions * CAP)] = arrived[sweep].reshape(regions * CAP, 8, 128)
        lookup[none] = edge[...]

        def pick(site, carry, sweep=sweep):
            for leg in range(3):
                flat = lookup[recv_src[3 * site + leg]]
                unflatten(flat, 3 * site + leg)
                if sweep == SWEEPS - 1:
                    for j in range(pieces):
                        msg_out[site, leg : leg + 1, 128 * j : 128 * (j + 1)] = flat[j : j + 1]
            return carry

        lax.fori_loop(0, sites, pick, 0)

    outer = ((0,), (0,))
    same = same_block(bond)
    pack_lane = lax.broadcasted_iota(jnp.int32, (16, 128), 1) // bond

    def factor(site, carry):
        left = split(current[3 * site][:, :bond])
        right = split(current[3 * site + 1][:, :bond])
        on_a = contract(left, split(tensors[site]), outer)
        swapped = unchunk(swap_axes(chunks(on_a), swaps.at[0], swaps.at[1], bond), bond)
        weights = contract(right, split(swapped), outer)
        weights = weights.astype(jnp.bfloat16).astype(jnp.float32)
        tiles = [
            jnp.where(same, jnp.concatenate([weights[:, 128 * j : 128 * (j + 1)]] * per, axis=0), 0.0)
            for j in range(pieces)
        ]
        spread = jnp.concatenate(tiles, axis=0).astype(jnp.bfloat16)
        wide = jnp.dot(projectors[site], spread, preferred_element_type=jnp.float32)
        wide = fold_lanes(wide)
        packed = wide[:16]
        for p in range(1, per):
            packed = jnp.where(pack_lane == p, wide[16 * p : 16 * (p + 1)], packed)
        factors[site] = packed.astype(jnp.bfloat16)
        return carry

    lax.fori_loop(0, sites, factor, 0)

    def gate_remote(other, slot):
        return pltpu.make_async_remote_copy(
            src_ref=gate_outbox.at[other],
            dst_ref=gate_arrived.at[slot],
            send_sem=gate_send_sem.at[other],
            recv_sem=gate_recv_sem.at[slot],
            device_id=(other, core),
            device_id_type=MESH,
        )

    def gate_send(step, carry):
        other = lax.rem(me + step, regions)
        gate_outbox[other] = factors[gate_index[other]]
        gate_remote(other, me).start()
        return carry

    lax.fori_loop(1, regions, gate_send, 0)
    gate_arrived[me] = jnp.zeros_like(gate_arrived[me])

    def gate_collect(step, carry):
        other = lax.rem(me + step, regions)
        gate_remote(other, me).wait_send()
        gate_remote(other, other).wait_recv()
        return carry

    lax.fori_loop(1, regions, gate_collect, 0)
    factors[pl.ds(sites, regions)] = gate_arrived[...]
    factors[sites + regions] = jnp.zeros_like(factors[0])

    def gate_pick(site, carry):
        half[site] = factors[gate_src[site]]
        return carry

    lax.fori_loop(0, sites, gate_pick, 0)
    both[core] = half[...]
    swap = to_mate(half, both.at[core], SWEEPS)
    swap.start()
    swap.wait()

    def update_remote(site):
        return pltpu.make_async_remote_copy(
            src_ref=update_outbox.at[site],
            dst_ref=update_inbox.at[site],
            send_sem=update_send_sem.at[site],
            recv_sem=update_recv_sem.at[site],
            device_id=(me, 1 - core),
            device_id_type=MESH,
        )

    def mixed(site, new_spin):
        total = jnp.zeros((16, 128), jnp.float32)
        for spin in range(2):
            first = gate[(4 * new_spin + core) * 2 + spin]
            second = gate[(4 * new_spin + 2 + core) * 2 + spin]
            total = total + jnp.where(pack_lane < per // 2, first, second) * both[
                spin, site
            ].astype(jnp.float32)
        total = total + pltpu.roll(total, 64, 1)
        matrix = jnp.concatenate([total[:, :bond], total[:, bond : 2 * bond]], axis=0)
        return diagonal(matrix)

    def multiply(site, carry):
        factor_pair = jnp.concatenate([mixed(site, 1 - core), mixed(site, core)], axis=0)
        product = contract(split(chunks(tensors[site])), split(factor_pair), ((1,), (1,)))
        for j in range(pieces):
            part = product[bond * j : bond * (j + 1)]
            update_outbox[site, :, 128 * j : 128 * (j + 1)] = part[:, :128].astype(jnp.bfloat16)
            own[site, :, 128 * j : 128 * (j + 1)] = part[:, 128:]
        update_remote(site).start()
        return carry

    lax.fori_loop(0, sites, multiply, 0)

    def gather(site, carry):
        update_remote(site).wait()
        total = own[site] + update_inbox[site].astype(jnp.float32)
        own[site] = total
        squares[site] = jnp.sum((total * total).reshape(bond // 8, 8, width), axis=0)
        return carry

    lax.fori_loop(0, sites, gather, 0)
    summed = jnp.sum(squares[...], axis=(1, 2), keepdims=True)
    norms[0] = jnp.broadcast_to(summed, (sites, 8, 128))
    swap = to_mate(norms.at[0], norms.at[1], SWEEPS + 1)
    swap.start()
    swap.wait()

    def finish(site, carry):
        mean = (norms[0, site] + norms[1, site])[0:1, 0:1] / (2 * bond**3)
        updated = own[site] * lax.rsqrt(mean + EPSILON)
        new_out[site] = jnp.where(gate_src[site] == sites + regions, tensors[site], updated)
        return carry

    lax.fori_loop(0, sites, finish, 0)


def whole(regions, send_index, recv_src, gate_index, gate_src, gate, tensors, projectors, edge):
    sites, bond, width = tensors.shape
    messages = 3 * sites
    dma = pltpu.SemaphoreType.DMA
    return pl.pallas_call(
        functools.partial(whole_kernel, regions),
        out_shape=(
            jax.ShapeDtypeStruct(tensors.shape, jnp.float32),
            jax.ShapeDtypeStruct((sites, 3, width), jnp.float32),
        ),
        in_specs=[SMEM] * 5 + [VMEM] * 3,
        out_specs=(VMEM, VMEM),
        scratch_shapes=[
            pltpu.VMEM((messages, bond, 128), jnp.float32),
            pltpu.VMEM((6, bond * width // 128, 128), jnp.float32),
            pltpu.VMEM((3, bond, 128), jnp.float32),
            pltpu.VMEM((SWEEPS, messages, 8, 128), jnp.float32),
            pltpu.VMEM((SWEEPS, messages, 8, 128), jnp.float32),
            pltpu.VMEM((messages + regions * CAP + 1, 8, 128), jnp.float32),
            pltpu.VMEM((SWEEPS, regions, CAP, 8, 128), jnp.float32),
            pltpu.VMEM((SWEEPS, regions, CAP, 8, 128), jnp.float32),
            pltpu.VMEM((sites + regions + 1, 16, 128), jnp.bfloat16),
            pltpu.VMEM((regions, 16, 128), jnp.bfloat16),
            pltpu.VMEM((regions, 16, 128), jnp.bfloat16),
            pltpu.VMEM((2, sites, 16, 128), jnp.bfloat16),
            pltpu.VMEM((sites, 16, 128), jnp.bfloat16),
            pltpu.VMEM(tensors.shape, jnp.float32),
            pltpu.VMEM(tensors.shape, jnp.bfloat16),
            pltpu.VMEM(tensors.shape, jnp.bfloat16),
            pltpu.VMEM((sites, 8, width), jnp.float32),
            pltpu.VMEM((2, sites, 8, 128), jnp.float32),
            dma((2 * SWEEPS + 4,)),
            dma((SWEEPS, regions)),
            dma((SWEEPS, regions)),
            dma((regions,)),
            dma((regions,)),
            dma((sites,)),
            dma((sites,)),
        ],
        compiler_params=pltpu.CompilerParams(
            collective_id=0, has_side_effects=True, vmem_limit_bytes=48 * 2**20
        ),
    )(send_index, recv_src, gate_index, gate_src, gate, tensors, projectors, edge)


def shards(
    site_tensors,
    projectors,
    gate_matrix,
    recv_src,
    cut_list,
    cut_dest,
    gate_src,
    gate_list,
    gate_dest,
):
    site_count = site_tensors.shape[0]
    bond_dim = site_tensors.shape[2]
    regions = lax.axis_size("region")
    my_region = lax.axis_index("region")
    edge = jnp.zeros((bond_dim * bond_dim,), jnp.float32).at[0].set(bond_dim).reshape(8, 128)
    own_dest = lax.dynamic_index_in_dim(cut_dest, my_region, 0, keepdims=False)
    own_gate = lax.dynamic_index_in_dim(gate_dest, my_region, 0, keepdims=False)
    send_index = slots(cut_list, own_dest, regions * CAP)
    gate_index = slots(gate_list, own_gate, regions * GCAP)
    new_sites, messages = whole(
        regions,
        send_index,
        recv_src.reshape(-1),
        gate_index,
        gate_src,
        gate_matrix.reshape(-1),
        site_tensors.reshape(site_count, bond_dim, -1),
        projectors.reshape(site_count, 2 * bond_dim, -1),
        edge,
    )
    return (new_sites.reshape(site_tensors.shape), messages)


def solution(mesh):
    return jax.shard_map(
        shards,
        mesh=mesh,
        in_specs=(
            P("region", "blk", None, None),
            P("region", None, None, None),
            P(),
            P("region", None),
            P("region"),
            P(),
            P("region"),
            P("region"),
            P(),
        ),
        out_specs=(P("region", "blk", None, None), P("region", None, None)),
        check_vma=False,
    )
```

time: 492 us -> 74.5 us (0.15); the launches traced: 484 us -> 74.2 us
  matrix products: 210 us -> 0 us
  blocking collectives: 141 us -> 0 us
  Pallas kernels: 0 us -> 65.9 us
  waiting for transfers between devices: 50.5 us -> 0 us
  local copies, waits for them, and re-layouts: 55.2 us -> 7.46 us
  between operations: 14.6 us -> 0.68 us
  other arithmetic: 12.3 us -> 0.17 us
    dot_general x21 -> x0, matrix products: 210 us -> none  [the longest x2 42.2 us: outgoing(): jnp.einsum('isabc,icd->isabd', tensors, incoming[:, 2], precision=HIGHEST)]
    all_gather x4 -> x0, blocking collectives: 138 us -> none  [the longest x2 99.2 us: shards(): everyone = lax.all_gather(leaving, 'region', axis=0, tiled=True)]
    pallas_call x0 -> x1, Pallas kernels: none -> 65.9 us  [whole(): pl.pallas_call(functools.partial(whole_kernel, regions), out_shape=(jax.S...]
    psum x2 -> x0, waiting for transfers between devices: 32 us -> none  [shards(): totals = lax.psum(outgoing(tensors, incoming), 'blk')]
    another operation x6 -> x0, local copies, waits for them, and re-layouts: 26.8 us -> none
    unnamed x4 -> x0, waiting for transfers between devices: 18.6 us -> none
    transpose x1 -> x0, local copies, waits for them, and re-layouts: 8.95 us -> none  [shards(): jnp.einsum('iuvc,iacn->iauvn', tensors[:, 0], own_old, precision=HIGHEST)]
    reshape x8 -> x2, local copies, waits for them, and re-layouts: 8.81 us -> 0.16 us  [the longest x1 0.08 us: shards(): gate_matrix.reshape(-1)]
  transfers between devices with their start and end apart: 3 -> 0, of which waited for: 3 -> 0; matrix products, arithmetic and copies ran while one was open for 1% -> 0% of each run, Pallas kernels for 0% -> 0%
where the time goes in v1:
time: 74.5 us; the launch traced here: 74.2 us
  Pallas kernels  65.9 us (88%)
  local copies, waits for them, and re-layouts  7.46 us (10%)
    pallas_call x1, Pallas kernels, whole(): pl.pallas_call(functools.partial(whole_kernel, regions), out_shape=(jax.S...  65.9 us
    unnamed x23, local copies, waits for them, and re-layouts  7.1 us

profile of v1, /device:TPU:0, one launch (start us, length us, event | category | flops | bytes accessed | tf_op | source)
XLA Modules:
  0.0 74.2 jit_solution(7509167343828540908)
XLA Ops:
  0.6 0.0 copy-start
  0.6 0.0 copy-start.5
  0.7 0.7 copy-done.5
  1.3 0.1 reshape.47.gate
  1.4 0.0 copy-done
  1.4 0.0 copy-start.7
  1.5 0.7 copy-done.7
  2.1 0.0 copy-start.8
  2.1 0.0 copy-start.9
  2.1 0.2 dynamic-slice_reduce_fusion
  2.3 0.5 copy-done.8
  2.8 0.0 copy-start.6
  2.8 0.1 fusion.gate_index
  2.9 0.0 copy-done.9
  2.9 0.1 select_reduce_fusion.send_index
  2.9 0.5 copy-done.6
  3.4 0.0 copy-start.3
  3.4 0.1 copy.17
  3.5 0.0 copy-start.4
  3.5 0.1 reshape.46.recv_src
  3.6 0.5 copy-done.3
  4.1 0.1 copy-done.4
  4.2 0.0 copy-start.1
  4.2 1.2 %copy-done.1 = f32[8,1,32,1024]{3,2,1,0:T(8,128)S(1)} copy-done((f32[8,1,32,1024]{3,2,1,0:T(8,128)S(1)}, f32[8,1,32,1024]{3,2,1,0:T(8,128)}, u32[]{:S(2)}) %copy-start.1) | copy-done | bytes 1048600
  5.4 0.0 copy-start.2
  5.4 1.2 %copy-done.2 = bf16[8,2,32,1024]{3,2,1,0:T(8,128)(2,1)S(1)} copy-done((bf16[8,2,32,1024]{3,2,1,0:T(8,128)(2,1)S(1)}, bf16[8,2,32,1024]{3,2,1,0:T(8,128)(2,1)}, u32[]{:S(2)}) %copy-start.2) | copy-done | bytes 1048600
  6.6 65.9 %shard_map.104 = (f32[8,32,1024]{2,1,0:T(8,128)S(1)}, f32[8,3,1024]{2,1,0:T(4,128)S(1)}) custom-call(s32[64]{0:T(128)S(1)} %select_reduce_fusion.send_index, s32[24]{0:T(128)S(1)} %reshape.46.recv_src, s32[16]{0:T(128)S(1)} %fusion.gate_index, s32[8]{0:T(128)S(1)} %copy-done.4, f32[16]{0:T(128)S(1)} %reshape.47.gate, f32[8,32,1024]{2,1,0:T(8,128)S(1)} %bitcast.7, ...), custom_call_target="tpu_custom_call" | custom-call | tf_op jit(solution)/shard_map/pallas_call | solution.py:399
  72.6 0.7 copy.19
  73.3 1.0 %copy.21 = f32[8,1,32,1024]{3,2,1,0:T(8,128)} copy(f32[8,1,32,1024]{3,2,1,0:T(8,128)S(1)} %bitcast.9) | data formatting | bytes 2097152
  (1 shorter events, 0.0 us)
Async XLA Ops:
  0.6 0.8 %copy-start = (s32[16,10]{1,0:T(8,128)S(1)}, s32[16,10]{1,0:T(8,128)}, u32[]{:S(2)}) copy-start(s32[16,10]{1,0:T(8,128)} %param.16) | copy-start | bytes 1924
  0.6 0.7 copy-start.5
  1.4 0.7 copy-start.7
  2.1 0.7 copy-start.8
  2.1 0.7 %copy-start.9 = (s32[10]{0:T(128)S(1)}, s32[10]{0:T(128)}, u32[]{:S(2)}) copy-start(s32[10]{0:T(128)} %param.15) | copy-start | bytes 124
  2.8 0.7 copy-start.6
  3.4 0.7 copy-start.3
  3.5 0.7 copy-start.4
  4.2 1.2 %copy-start.1 = (f32[8,1,32,1024]{3,2,1,0:T(8,128)S(1)}, f32[8,1,32,1024]{3,2,1,0:T(8,128)}, u32[]{:S(2)}) copy-start(f32[8,1,32,1024]{3,2,1,0:T(8,128)} %param.11) | copy-start | bytes 3145732
  5.4 1.2 %copy-start.2 = (bf16[8,2,32,1024]{3,2,1,0:T(8,128)(2,1)S(1)}, bf16[8,2,32,1024]{3,2,1,0:T(8,128)(2,1)}, u32[]{:S(2)}) copy-start(bf16[8,2,32,1024]{3,2,1,0:T(8,128)(2,1)} %param.12) | copy-start | bytes 3145732

commit v2 on v1

--- a/solution.py
+++ b/solution.py
@@ -12,6 +12,7 @@
 GCAP = 1
 EPSILON = 1e-06
 VMEM = pl.BlockSpec(memory_space=pltpu.VMEM)
+HBM = pl.BlockSpec(memory_space=pltpu.HBM)
 SMEM = pl.BlockSpec(memory_space=pltpu.SMEM)
 MESH = pl.DeviceIdType.MESH
 
@@ -107,6 +108,32 @@
     return leg_zero, leg_one, fold_lanes(folded)[:, :bond]
 
 
+def first_terms(tensors, opens, site, swaps):
+    bond, width = tensors.shape[1:]
+    inner, outer = ((1,), (1,)), ((0,), (0,))
+    wide = tensors[site]
+    plain = chunks(wide)
+    swapped = unchunk(swap_axes(plain, swaps.at[0], swaps.at[1], bond), bond)
+    row = lax.broadcasted_iota(jnp.int32, wide.shape, 0)
+    lane = lax.broadcasted_iota(jnp.int32, wide.shape, 1)
+
+    def scaled(value, index, leg):
+        edge = jnp.where(index == 0, float(bond) * value, 0.0)
+        return jnp.where(opens[leg], edge, value)
+
+    on_a = split(chunks(scaled(wide, row, 0)))
+    on_b_wide = scaled(wide, lane // bond, 1)
+    on_b = split(chunks(on_b_wide))
+    on_c = split(scaled(wide, lane % bond, 2))
+    leg_zero = contract(split(on_b_wide), on_c, inner)
+    on_a_swapped = split(scaled(swapped, lane // bond, 0))
+    on_c_swapped = split(scaled(swapped, lane % bond, 2))
+    leg_one = contract(on_a_swapped, on_c_swapped, inner)
+    crossed = jnp.where(same_block(bond), contract(on_a, on_b, outer), 0.0)
+    folded = sum(crossed[bond * p : bond * (p + 1)] for p in range(128 // bond))
+    return leg_zero, leg_one, fold_lanes(folded)[:, :bond]
+
+
 def same_block(bond):
     row = lax.broadcasted_iota(jnp.int32, (128, 128), 0) // bond
     column = lax.broadcasted_iota(jnp.int32, (128, 128), 1) // bond
@@ -131,16 +158,16 @@
 
 def whole_kernel(
     regions,
-    send_index,
-    recv_src,
-    gate_index,
-    gate_src,
+    table,
     gate,
+    tensors_far,
+    projectors_far,
+    new_out,
+    msg_out,
     tensors,
     projectors,
-    edge,
-    new_out,
-    msg_out,
+    first_outbox,
+    first_arrived,
     current,
     swaps,
     flats,
@@ -166,6 +193,7 @@
     gate_recv_sem,
     update_send_sem,
     update_recv_sem,
+    load_sem,
 ):
     me = lax.axis_index("region")
     core = lax.axis_index("blk")
@@ -174,6 +202,26 @@
     pieces = width // 128
     messages = 3 * sites
     none = messages + regions * CAP
+
+    def send_index(entry):
+        return table[entry]
+
+    def gate_index(entry):
+        return table[regions * CAP + entry]
+
+    def recv_src(entry):
+        return table[regions * (CAP + GCAP) + entry]
+
+    def gate_src(entry):
+        return table[regions * (CAP + GCAP) + messages + entry]
+
+    def load(site):
+        return pltpu.make_async_copy(tensors_far.at[site], tensors.at[site], load_sem.at[site])
+
+    load_projectors = pltpu.make_async_copy(projectors_far, projectors, load_sem.at[sites])
+    for site in range(sites):
+        load(site).start()
+    load_projectors.start()
     barrier = pltpu.get_barrier_semaphore()
     pl.semaphore_signal(barrier, inc=1, device_id=(me, 1 - core), device_id_type=MESH)
 
@@ -203,23 +251,27 @@
     column = lax.broadcasted_iota(jnp.int32, (8, 128), 1)
     place = 128 * row + column
     diagonal_flat = (place // bond) == (place % bond)
-    identity = jnp.where(diagonal_flat, 1.0, 0.0).astype(jnp.float32)
-
-    def begin(entry, carry):
-        unflatten(jnp.where(recv_src[entry] == none, edge[...], identity), entry)
-        return carry
-
-    lax.fori_loop(0, messages, begin, 0)
+    edge = jnp.where(place == 0, float(bond), 0.0)
 
     for sweep in range(SWEEPS):
 
-        def terms(site, carry, sweep=sweep):
-            legs = site_terms(tensors, current, site, swaps)
-            for leg in range(3):
-                partial[sweep, 3 * site + leg] = flatten(legs[leg], flats.at[leg])
+        def terms(pair, carry, sweep=sweep):
+            for lane in range(2):
+                site = 2 * pair + lane
+                if sweep == 0:
+                    load(site).wait()
+            for lane in range(2):
+                site = 2 * pair + lane
+                if sweep == 0:
+                    opens = [recv_src(3 * site + leg) == none for leg in range(3)]
+                    legs = first_terms(tensors, opens, site, swaps.at[lane])
+                else:
+                    legs = site_terms(tensors, current, site, swaps.at[lane])
+                for leg in range(3):
+                    partial[sweep, 3 * site + leg] = flatten(legs[leg], flats.at[lane, leg])
             return carry
 
-        lax.fori_loop(0, sites, terms, 0)
+        lax.fori_loop(0, sites // 2, terms, 0)
         if sweep == 0:
             pl.semaphore_wait(barrier, regions)
         swap = to_mate(partial.at[sweep], mate.at[sweep], sweep)
@@ -231,8 +283,8 @@
 
         def remote(other, slot, sweep=sweep):
             return pltpu.make_async_remote_copy(
-                src_ref=outbox.at[sweep, other],
-                dst_ref=arrived.at[sweep, slot],
+                src_ref=first_outbox.at[other] if sweep == 0 else outbox.at[other],
+                dst_ref=first_arrived.at[slot] if sweep == 0 else arrived.at[slot],
                 send_sem=send_sem.at[sweep, other],
                 recv_sem=recv_sem.at[sweep, slot],
                 device_id=(other, core),
@@ -241,13 +293,19 @@
 
         def send(step, carry, sweep=sweep, remote=remote):
             other = lax.rem(me + step, regions)
-            for slot in range(CAP):
-                outbox[sweep, other, slot] = lookup[send_index[CAP * other + slot]]
+            leaving = jnp.concatenate(
+                [lookup[send_index(CAP * other + slot)] for slot in range(CAP)], axis=0
+            )
+            if sweep == 0:
+                first_outbox[other] = leaving.astype(jnp.bfloat16)
+            else:
+                outbox[other] = leaving
             remote(other, me).start()
             return carry
 
         lax.fori_loop(1, regions, send, 0)
-        arrived[sweep, me] = jnp.zeros_like(arrived[sweep, me])
+        landed = first_arrived if sweep == 0 else arrived
+        landed[me] = jnp.zeros_like(landed[me])
 
         def collect(step, carry, remote=remote):
             other = lax.rem(me + step, regions)
@@ -256,12 +314,14 @@
             return carry
 
         lax.fori_loop(1, regions, collect, 0)
-        lookup[pl.ds(messages, regions * CAP)] = arrived[sweep].reshape(regions * CAP, 8, 128)
-        lookup[none] = edge[...]
+        lookup[pl.ds(messages, regions * CAP)] = (
+            landed[...].astype(jnp.float32).reshape(regions * CAP, 8, 128)
+        )
+        lookup[none] = edge
 
         def pick(site, carry, sweep=sweep):
             for leg in range(3):
-                flat = lookup[recv_src[3 * site + leg]]
+                flat = lookup[recv_src(3 * site + leg)]
                 unflatten(flat, 3 * site + leg)
                 if sweep == SWEEPS - 1:
                     for j in range(pieces):
@@ -274,11 +334,13 @@
     same = same_block(bond)
     pack_lane = lax.broadcasted_iota(jnp.int32, (16, 128), 1) // bond
 
-    def factor(site, carry):
+    load_projectors.wait()
+
+    def factor(site, scratch):
         left = split(current[3 * site][:, :bond])
         right = split(current[3 * site + 1][:, :bond])
         on_a = contract(left, split(tensors[site]), outer)
-        swapped = unchunk(swap_axes(chunks(on_a), swaps.at[0], swaps.at[1], bond), bond)
+        swapped = unchunk(swap_axes(chunks(on_a), scratch.at[0], scratch.at[1], bond), bond)
         weights = contract(right, split(swapped), outer)
         weights = weights.astype(jnp.bfloat16).astype(jnp.float32)
         tiles = [
@@ -292,9 +354,13 @@
         for p in range(1, per):
             packed = jnp.where(pack_lane == p, wide[16 * p : 16 * (p + 1)], packed)
         factors[site] = packed.astype(jnp.bfloat16)
-        return carry
-
-    lax.fori_loop(0, sites, factor, 0)
+
+    def factor_pair(pair, carry):
+        for lane in range(2):
+            factor(2 * pair + lane, swaps.at[lane])
+        return carry
+
+    lax.fori_loop(0, sites // 2, factor_pair, 0)
 
     def gate_remote(other, slot):
         return pltpu.make_async_remote_copy(
@@ -308,7 +374,7 @@
 
     def gate_send(step, carry):
         other = lax.rem(me + step, regions)
-        gate_outbox[other] = factors[gate_index[other]]
+        gate_outbox[other] = factors[gate_index(other)]
         gate_remote(other, me).start()
         return carry
 
@@ -326,7 +392,7 @@
     factors[sites + regions] = jnp.zeros_like(factors[0])
 
     def gate_pick(site, carry):
-        half[site] = factors[gate_src[site]]
+        half[site] = factors[gate_src(site)]
         return carry
 
     lax.fori_loop(0, sites, gate_pick, 0)
@@ -386,13 +452,13 @@
     def finish(site, carry):
         mean = (norms[0, site] + norms[1, site])[0:1, 0:1] / (2 * bond**3)
         updated = own[site] * lax.rsqrt(mean + EPSILON)
-        new_out[site] = jnp.where(gate_src[site] == sites + regions, tensors[site], updated)
+        new_out[site] = jnp.where(gate_src(site) == sites + regions, tensors[site], updated)
         return carry
 
     lax.fori_loop(0, sites, finish, 0)
 
 
-def whole(regions, send_index, recv_src, gate_index, gate_src, gate, tensors, projectors, edge):
+def whole(regions, table, gate, tensors, projectors):
     sites, bond, width = tensors.shape
     messages = 3 * sites
     dma = pltpu.SemaphoreType.DMA
@@ -402,17 +468,21 @@
             jax.ShapeDtypeStruct(tensors.shape, jnp.float32),
             jax.ShapeDtypeStruct((sites, 3, width), jnp.float32),
         ),
-        in_specs=[SMEM] * 5 + [VMEM] * 3,
+        in_specs=[SMEM] * 2 + [HBM] * 2,
         out_specs=(VMEM, VMEM),
         scratch_shapes=[
+            pltpu.VMEM(tensors.shape, jnp.float32),
+            pltpu.VMEM(projectors.shape, jnp.bfloat16),
+            pltpu.VMEM((regions, CAP * 8, 128), jnp.bfloat16),
+            pltpu.VMEM((regions, CAP * 8, 128), jnp.bfloat16),
             pltpu.VMEM((messages, bond, 128), jnp.float32),
-            pltpu.VMEM((6, bond * width // 128, 128), jnp.float32),
-            pltpu.VMEM((3, bond, 128), jnp.float32),
+            pltpu.VMEM((2, 6, bond * width // 128, 128), jnp.float32),
+            pltpu.VMEM((2, 3, bond, 128), jnp.float32),
             pltpu.VMEM((SWEEPS, messages, 8, 128), jnp.float32),
             pltpu.VMEM((SWEEPS, messages, 8, 128), jnp.float32),
             pltpu.VMEM((messages + regions * CAP + 1, 8, 128), jnp.float32),
-            pltpu.VMEM((SWEEPS, regions, CAP, 8, 128), jnp.float32),
-            pltpu.VMEM((SWEEPS, regions, CAP, 8, 128), jnp.float32),
+            pltpu.VMEM((regions, CAP * 8, 128), jnp.float32),
+            pltpu.VMEM((regions, CAP * 8, 128), jnp.float32),
             pltpu.VMEM((sites + regions + 1, 16, 128), jnp.bfloat16),
             pltpu.VMEM((regions, 16, 128), jnp.bfloat16),
             pltpu.VMEM((regions, 16, 128), jnp.bfloat16),
@@ -430,11 +500,12 @@
             dma((regions,)),
             dma((sites,)),
             dma((sites,)),
+            dma((sites + 1,)),
         ],
         compiler_params=pltpu.CompilerParams(
             collective_id=0, has_side_effects=True, vmem_limit_bytes=48 * 2**20
         ),
-    )(send_index, recv_src, gate_index, gate_src, gate, tensors, projectors, edge)
+    )(table, gate, tensors, projectors)
 
 
 def shards(
@@ -452,21 +523,17 @@
     bond_dim = site_tensors.shape[2]
     regions = lax.axis_size("region")
     my_region = lax.axis_index("region")
-    edge = jnp.zeros((bond_dim * bond_dim,), jnp.float32).at[0].set(bond_dim).reshape(8, 128)
     own_dest = lax.dynamic_index_in_dim(cut_dest, my_region, 0, keepdims=False)
     own_gate = lax.dynamic_index_in_dim(gate_dest, my_region, 0, keepdims=False)
     send_index = slots(cut_list, own_dest, regions * CAP)
     gate_index = slots(gate_list, own_gate, regions * GCAP)
+    table = jnp.concatenate([send_index, gate_index, recv_src.reshape(-1), gate_src])
     new_sites, messages = whole(
         regions,
-        send_index,
-        recv_src.reshape(-1),
-        gate_index,
-        gate_src,
+        table,
         gate_matrix.reshape(-1),
         site_tensors.reshape(site_count, bond_dim, -1),
         projectors.reshape(site_count, 2 * bond_dim, -1),
-        edge,
     )
     return (new_sites.reshape(site_tensors.shape), messages)
 

time: 74.5 us -> 62.6 us (0.84)
  Pallas kernels: 65.9 us -> 53.9 us
    pallas_call x1, Pallas kernels: 65.9 us -> 53.9 us  [whole(): pl.pallas_call(functools.partial(whole_kernel, regions), out_shape=(jax.S...]
    unnamed x23 -> x21, local copies, waits for them, and re-layouts: 7.1 us -> 7.1 us
where the time goes in v2:
time: 62.6 us; the launch traced here: 62.3 us
  Pallas kernels  53.9 us (86%)
  local copies, waits for them, and re-layouts  7.46 us (12%)
  between operations  0.68 us (1%)
    pallas_call x1, Pallas kernels, whole(): pl.pallas_call(functools.partial(whole_kernel, regions), out_shape=(jax.S...  53.9 us
    unnamed x21, local copies, waits for them, and re-layouts  7.1 us

profile of v2, /device:TPU:0, one launch (start us, length us, event | category | flops | bytes accessed | tf_op | source)
XLA Modules:
  0.0 62.3 jit_solution(7942082736403902301)
XLA Ops:
  0.6 0.0 copy-start
  0.6 0.0 copy-start.3
  0.7 0.7 %copy-done.3 = f32[2,2,2,2]{3,2,1,0:T(2,128)S(1)} copy-done((f32[2,2,2,2]{3,2,1,0:T(2,128)S(1)}, f32[2,2,2,2]{3,2,1,0:T(2,128)}, u32[]{:S(2)}) %copy-start.3) | copy-done | bytes 88
  1.3 0.1 reshape.22.gate
  1.4 0.0 copy-done
  1.4 0.0 copy-start.5
  1.5 0.7 %copy-done.5 = s32[16,2]{0,1:T(2,128)S(1)} copy-done((s32[16,2]{0,1:T(2,128)S(1)}, s32[16,2]{0,1:T(2,128)}, u32[]{:S(2)}) %copy-start.5) | copy-done | bytes 152
  2.1 0.0 copy-start.7
  2.1 0.0 copy-start.8
  2.1 0.2 dynamic-slice_reduce_fusion
  2.3 0.5 copy-done.7
  2.8 0.0 copy-start.4
  2.8 0.1 fusion
  2.9 0.0 copy-done.8
  2.9 0.1 select_reduce_fusion
  2.9 0.5 copy-done.4
  3.4 0.1 copy.17
  3.5 0.0 copy-start.6
  3.5 0.1 reshape.21
  3.6 0.6 copy-done.6
  4.2 0.1 pad_add_fusion.table
  4.3 0.0 copy-start.1
  4.3 1.2 %copy-done.1 = f32[8,1,32,1024]{3,2,1,0:T(8,128)S(1)} copy-done((f32[8,1,32,1024]{3,2,1,0:T(8,128)S(1)}, f32[8,1,32,1024]{3,2,1,0:T(8,128)}, u32[]{:S(2)}) %copy-start.1) | copy-done | bytes 1048600
  5.5 0.0 copy-start.2
  5.5 1.2 %copy-done.2 = bf16[8,2,32,1024]{3,2,1,0:T(8,128)(2,1)S(1)} copy-done((bf16[8,2,32,1024]{3,2,1,0:T(8,128)(2,1)S(1)}, bf16[8,2,32,1024]{3,2,1,0:T(8,128)(2,1)}, u32[]{:S(2)}) %copy-start.2) | copy-done | bytes 1048600
  6.7 53.9 %shard_map.104 = (f32[8,32,1024]{2,1,0:T(8,128)S(1)}, f32[8,3,1024]{2,1,0:T(4,128)S(1)}) custom-call(s32[112]{0:T(128)S(1)} %pad_add_fusion.table, f32[16]{0:T(128)S(1)} %reshape.22.gate, f32[8,32,1024]{2,1,0:T(8,128)S(1)} %bitcast.8, bf16[8,64,1024]{2,1,0:T(8,128)(2,1)S(1)} %bitcast.9), custom_call_target="tpu_custom_call" | custom-call | tf_op jit(solution)/shard_map/pallas_call | solution.py:465
  60.7 0.7 %copy.19 = f32[8,3,1024]{2,0,1:T(8,128)} copy(f32[8,3,1024]{2,1,0:T(4,128)S(1)} %get-tuple-element.11) | data formatting | bytes 196608
  61.4 1.0 %copy.21 = f32[8,1,32,1024]{3,2,1,0:T(8,128)} copy(f32[8,1,32,1024]{3,2,1,0:T(8,128)S(1)} %bitcast.7) | data formatting | bytes 2097152
  (1 shorter events, 0.0 us)
Async XLA Ops:
  0.6 0.8 %copy-start = (s32[16,10]{1,0:T(8,128)S(1)}, s32[16,10]{1,0:T(8,128)}, u32[]{:S(2)}) copy-start(s32[16,10]{1,0:T(8,128)} %param.14) | copy-start | bytes 1924
  0.6 0.7 %copy-start.3 = (f32[2,2,2,2]{3,2,1,0:T(2,128)S(1)}, f32[2,2,2,2]{3,2,1,0:T(2,128)}, u32[]{:S(2)}) copy-start(f32[2,2,2,2]{3,2,1,0:T(2,128)} %param.11) | copy-start | bytes 196
  1.4 0.7 %copy-start.5 = (s32[16,2]{0,1:T(2,128)S(1)}, s32[16,2]{0,1:T(2,128)}, u32[]{:S(2)}) copy-start(s32[16,2]{0,1:T(2,128)} %param.17) | copy-start | bytes 388
  2.1 0.7 %copy-start.7 = (s32[2]{0:T(128)S(1)}, s32[2]{0:T(128)}, u32[]{:S(2)}) copy-start(s32[2]{0:T(128)} %param.16) | copy-start | bytes 28
  2.1 0.7 %copy-start.8 = (s32[10]{0:T(128)S(1)}, s32[10]{0:T(128)}, u32[]{:S(2)}) copy-start(s32[10]{0:T(128)} %param.13) | copy-start | bytes 124
  2.8 0.7 %copy-start.4 = (s32[8,3]{0,1:T(4,128)S(1)}, s32[8,3]{0,1:T(4,128)}, u32[]{:S(2)}) copy-start(s32[8,3]{0,1:T(4,128)} %param.12) | copy-start | bytes 292
  3.5 0.7 %copy-start.6 = (s32[8]{0:T(128)S(1)}, s32[8]{0:T(128)}, u32[]{:S(2)}) copy-start(s32[8]{0:T(128)} %param.15) | copy-start | bytes 100
  4.3 1.2 %copy-start.1 = (f32[8,1,32,1024]{3,2,1,0:T(8,128)S(1)}, f32[8,1,32,1024]{3,2,1,0:T(8,128)}, u32[]{:S(2)}) copy-start(f32[8,1,32,1024]{3,2,1,0:T(8,128)} %param.9) | copy-start | bytes 3145732
  5.5 1.2 %copy-start.2 = (bf16[8,2,32,1024]{3,2,1,0:T(8,128)(2,1)S(1)}, bf16[8,2,32,1024]{3,2,1,0:T(8,128)(2,1)}, u32[]{:S(2)}) copy-start(bf16[8,2,32,1024]{3,2,1,0:T(8,128)(2,1)} %param.10) | copy-start | bytes 3145732

commit v3 on v2

--- a/solution.py
+++ b/solution.py
@@ -423,7 +423,7 @@
         matrix = jnp.concatenate([total[:, :bond], total[:, bond : 2 * bond]], axis=0)
         return diagonal(matrix)
 
-    def multiply(site, carry):
+    def multiply(site):
         factor_pair = jnp.concatenate([mixed(site, 1 - core), mixed(site, core)], axis=0)
         product = contract(split(chunks(tensors[site])), split(factor_pair), ((1,), (1,)))
         for j in range(pieces):
@@ -431,9 +431,13 @@
             update_outbox[site, :, 128 * j : 128 * (j + 1)] = part[:, :128].astype(jnp.bfloat16)
             own[site, :, 128 * j : 128 * (j + 1)] = part[:, 128:]
         update_remote(site).start()
-        return carry
-
-    lax.fori_loop(0, sites, multiply, 0)
+
+    def multiply_pair(pair, carry):
+        for lane in range(2):
+            multiply(2 * pair + lane)
+        return carry
+
+    lax.fori_loop(0, sites // 2, multiply_pair, 0)
 
     def gather(site, carry):
         update_remote(site).wait()
@@ -503,7 +507,7 @@
             dma((sites + 1,)),
         ],
         compiler_params=pltpu.CompilerParams(
-            collective_id=0, has_side_effects=True, vmem_limit_bytes=48 * 2**20
+            collective_id=0, has_side_effects=True, vmem_limit_bytes=60 * 2**20
         ),
     )(table, gate, tensors, projectors)
 

time: 62.6 us -> 64.6 us (1.032)
  Pallas kernels: 53.9 us -> 55.1 us
    pallas_call x1, Pallas kernels: 53.9 us -> 55.1 us  [whole(): pl.pallas_call(functools.partial(whole_kernel, regions), out_shape=(jax.S...]
    unnamed x21 -> x17, local copies, waits for them, and re-layouts: 7.1 us -> 6.91 us
where the time goes in v3:
time: 64.6 us; the launch traced here: 64.3 us
  Pallas kernels  55.1 us (85%)
  local copies, waits for them, and re-layouts  7.77 us (12%)
  other arithmetic  0.76 us (1%)
  between operations  0.67 us (1%)
    pallas_call x1, Pallas kernels, whole(): pl.pallas_call(functools.partial(whole_kernel, regions), out_shape=(jax.S...  55.1 us
    unnamed x17, local copies, waits for them, and re-layouts  6.91 us

profile of v3, /device:TPU:0, one launch (start us, length us, event | category | flops | bytes accessed | tf_op | source)
XLA Modules:
  0.0 64.3 jit_solution(10728419291170611354)
XLA Ops:
  0.6 0.0 copy-start
  0.6 0.0 copy-start.1
  0.7 0.7 %copy-done.1 = f32[2,2,2,2]{3,2,1,0:T(2,128)S(1)} copy-done((f32[2,2,2,2]{3,2,1,0:T(2,128)S(1)}, f32[2,2,2,2]{3,2,1,0:T(2,128)}, u32[]{:S(2)}) %copy-start.1) | copy-done | bytes 88
  1.3 0.6 reshape.22.gate
  1.9 0.0 copy-done
  1.9 0.0 copy-start.3
  1.9 0.7 %copy-done.3 = s32[16,2]{0,1:T(2,128)S(1)} copy-done((s32[16,2]{0,1:T(2,128)S(1)}, s32[16,2]{0,1:T(2,128)}, u32[]{:S(2)}) %copy-start.3) | copy-done | bytes 152
  2.6 0.0 copy-start.5
  2.6 0.0 copy-start.6
  2.6 0.2 dynamic-slice_reduce_fusion
  2.8 0.5 copy-done.5
  3.3 0.0 copy-start.2
  3.3 0.1 fusion
  3.4 0.0 copy-done.6
  3.4 0.1 select_reduce_fusion
  3.5 0.5 copy-done.2
  4.0 0.1 copy.17
  4.0 0.0 copy-start.4
  4.0 0.1 reshape.21
  4.1 0.6 copy-done.4
  4.7 0.6 pad_add_fusion.table
  5.3 55.1 %shard_map.104 = (f32[8,32,1024]{2,1,0:T(8,128)}, f32[8,3,1024]{2,1,0:T(4,128)}) custom-call(s32[112]{0:T(128)} %pad_add_fusion.table, f32[16]{0:T(128)} %reshape.22.gate, f32[8,32,1024]{2,1,0:T(8,128)} %bitcast.8, bf16[8,64,1024]{2,1,0:T(8,128)(2,1)} %bitcast.9), custom_call_target="tpu_custom_call" | custom-call | tf_op jit(solution)/shard_map/pallas_call | solution.py:469
  60.4 1.6 %copy.19 = f32[8,3,1024]{2,0,1:T(8,128)} copy(f32[8,3,1024]{2,1,0:T(4,128)} %get-tuple-element.11) | data formatting | bytes 196608
  62.0 2.3 %copy.21 = f32[8,1,32,1024]{3,2,1,0:T(8,128)} copy(f32[8,1,32,1024]{3,2,1,0:T(8,128)} %bitcast.7) | data formatting | bytes 2097152
  (1 shorter events, 0.0 us)
Async XLA Ops:
  0.6 1.3 %copy-start = (s32[16,10]{1,0:T(8,128)S(1)}, s32[16,10]{1,0:T(8,128)}, u32[]{:S(2)}) copy-start(s32[16,10]{1,0:T(8,128)} %param.14) | copy-start | bytes 1924
  0.6 0.7 %copy-start.1 = (f32[2,2,2,2]{3,2,1,0:T(2,128)S(1)}, f32[2,2,2,2]{3,2,1,0:T(2,128)}, u32[]{:S(2)}) copy-start(f32[2,2,2,2]{3,2,1,0:T(2,128)} %param.11) | copy-start | bytes 196
  1.9 0.7 %copy-start.3 = (s32[16,2]{0,1:T(2,128)S(1)}, s32[16,2]{0,1:T(2,128)}, u32[]{:S(2)}) copy-start(s32[16,2]{0,1:T(2,128)} %param.17) | copy-start | bytes 388
  2.6 0.7 %copy-start.5 = (s32[2]{0:T(128)S(1)}, s32[2]{0:T(128)}, u32[]{:S(2)}) copy-start(s32[2]{0:T(128)} %param.16) | copy-start | bytes 28
  2.6 0.7 %copy-start.6 = (s32[10]{0:T(128)S(1)}, s32[10]{0:T(128)}, u32[]{:S(2)}) copy-start(s32[10]{0:T(128)} %param.13) | copy-start | bytes 124
  3.3 0.7 %copy-start.2 = (s32[8,3]{0,1:T(4,128)S(1)}, s32[8,3]{0,1:T(4,128)}, u32[]{:S(2)}) copy-start(s32[8,3]{0,1:T(4,128)} %param.12) | copy-start | bytes 292
  4.0 0.7 %copy-start.4 = (s32[8]{0:T(128)S(1)}, s32[8]{0:T(128)}, u32[]{:S(2)}) copy-start(s32[8]{0:T(128)} %param.15) | copy-start | bytes 100
